TPU v7x, 32 devices: a whole 2x2x4 slice. The times are simulated.
32 devices in a mesh: groups: 2 (over y), pool: 4 (over z), ffn: 2 (over x), sub: 2 (over core).
Axes of the slice: x: 2, y: 2, z: 4, core: 2. Of those that a mesh axis runs over, the one named last changes fastest.
Arguments:
- queries: bfloat16 [256, 8192], P(('groups', 'pool'), ('ffn', 'sub')), parts along dimension 0, may hold values from -200 to 200
- cache_keys: bfloat16 [256, 128, 1024], P(('groups', 'pool'), None, ('ffn', 'sub')), parts along dimension 0, may hold values from -6 to 6
- cache_values: bfloat16 [256, 128, 1024], P(('groups', 'pool'), None, ('ffn', 'sub')), parts along dimension 0, may hold values from -6 to 6
- new_keys: bfloat16 [256, 1024], P(('groups', 'pool'), ('ffn', 'sub')), parts along dimension 0, may hold values from -6 to 6
- new_values: bfloat16 [256, 1024], P(('groups', 'pool'), ('ffn', 'sub')), parts along dimension 0, may hold values from -6 to 6
- kv_lengths: int32 [256], P(('groups', 'pool')), parts along dimension 0, may hold values from 1 to 128, 8192 in all
- residual: float32 [256, 8192], P(('groups', 'pool'), ('ffn', 'sub')), parts along dimension 0, may hold values from -200 to 200
- norm_gain: float32 [8192], P(('ffn', 'sub')), may hold values from 0.1 to 1.9
- gate_weight: bfloat16 [8192, 14336], P(('ffn', 'sub'), 'pool'), may hold values from -0.0625 to 0.0625
- up_weight: bfloat16 [8192, 14336], P(('ffn', 'sub'), 'pool'), may hold values from -0.0625 to 0.0625
- down_weight: bfloat16 [14336, 8192], P('pool', ('ffn', 'sub')), may hold values from -0.046875 to 0.046875
Outputs:
- layer_out: float32 [256, 8192], P(('groups', 'pool'), ('ffn', 'sub')), parts along dimension 0
There are 2 independent parts, one for each index of `groups`. A program takes and returns all parts, laid end to end along the dimension named above; an argument that names none is the same for every part. Nothing has to cross between parts.
Inputs may be any that keep to these rules, and one draw needn't show every extreme that they name: `kv_lengths`: the lengths of one part sum to 128 * 128 // 2 (the total is per part, not over all parts).
All inputs are finite; a program needn't handle non-finite values. No bound on the sum of `kv_lengths` on one device may be relied on, other than what follows from the above.
Results may differ from a plain program's by a relative error of at most 0.0035.
Values may be sent and summed in bfloat16 or wider, within the bound.
A program may use at most 128 MiB of HBM per device.

v0:
```python
import math

import jax
import jax.numpy as jnp
from jax import lax
from jax.sharding import PartitionSpec as P

HEAD_DIM = 128
D = 8192


def rounded(values):
    return lax.optimization_barrier(values.astype(jnp.bfloat16)).astype(jnp.float32)


def attend(queries, cache_keys, cache_values, new_keys, new_values, kv_lengths):
    row_count, cap_len, kv_width = cache_keys.shape
    kv_local = kv_width // HEAD_DIM
    group_size = queries.shape[1] // kv_width
    scaling = 1.0 / math.sqrt(HEAD_DIM)
    query_heads = queries.reshape(row_count, kv_local, group_size, HEAD_DIM)
    key_heads = cache_keys.reshape(row_count, cap_len, kv_local, HEAD_DIM)
    value_heads = cache_values.reshape(row_count, cap_len, kv_local, HEAD_DIM)
    scores = (
        jnp.einsum("rhgd,rchd->rhgc", query_heads, key_heads, preferred_element_type=jnp.float32)
        * scaling
    )
    self_score = (
        jnp.einsum(
            "rhgd,rhd->rhg",
            query_heads,
            new_keys.reshape(row_count, kv_local, HEAD_DIM),
            preferred_element_type=jnp.float32,
        )
        * scaling
    )
    live_mask = lax.broadcasted_iota(jnp.int32, (row_count, cap_len), 1) < kv_lengths[:, None]
    scores = jnp.where(live_mask[:, None, None, :], scores, -jnp.inf)
    largest = jnp.maximum(jnp.max(scores, axis=3), self_score)
    expo = jnp.exp(scores - largest[..., None])
    self_expo = jnp.exp(self_score - largest)
    totals = jnp.sum(expo, axis=3) + self_expo
    mixed = jnp.einsum(
        "rhgc,rchd->rhgd",
        expo.astype(jnp.bfloat16),
        value_heads,
        preferred_element_type=jnp.float32,
    )
    mixed = mixed + rounded(self_expo)[..., None] * new_values.reshape(
        row_count, kv_local, 1, HEAD_DIM
    ).astype(jnp.float32)
    return (mixed / totals[..., None]).reshape(row_count, kv_local * group_size * HEAD_DIM)


def layer_rows(
    queries,
    cache_keys,
    cache_values,
    new_keys,
    new_values,
    kv_lengths,
    residual,
    norm_gain,
    gate_weight,
    up_weight,
    down_weight,
):
    hidden_state = residual + attend(
        queries, cache_keys, cache_values, new_keys, new_values, kv_lengths
    )
    squares = lax.psum(jnp.sum(hidden_state * hidden_state, axis=1), ("ffn", "sub"))
    normed = (hidden_state * lax.rsqrt(squares / D + 1e-05)[:, None] * norm_gain[None, :]).astype(
        jnp.bfloat16
    )
    unit_width = gate_weight.shape[1]
    block_rows = lax.all_gather(normed, "pool", axis=0, tiled=True)
    gate_part = jnp.dot(block_rows, gate_weight, preferred_element_type=jnp.float32)
    up_part = jnp.dot(block_rows, up_weight, preferred_element_type=jnp.float32)
    partial_value = jnp.concatenate([gate_part, up_part], axis=1)
    summed = lax.psum(partial_value.astype(jnp.bfloat16), ("ffn", "sub")).astype(jnp.float32)
    hidden_units = (jax.nn.silu(summed[:, :unit_width]) * summed[:, unit_width:]).astype(
        jnp.bfloat16
    )
    ffn_total = lax.psum_scatter(
        jnp.dot(hidden_units, down_weight, preferred_element_type=jnp.float32).astype(jnp.bfloat16),
        "pool",
        scatter_dimension=0,
        tiled=True,
    ).astype(jnp.float32)
    return hidden_state + ffn_total


def on_device(
    queries,
    cache_keys,
    cache_values,
    new_keys,
    new_values,
    kv_lengths,
    residual,
    norm_gain,
    gate_weight,
    up_weight,
    down_weight,
):
    return layer_rows(
        queries,
        cache_keys,
        cache_values,
        new_keys,
        new_values,
        kv_lengths,
        residual,
        norm_gain,
        gate_weight,
        up_weight,
        down_weight,
    )


def solution(mesh):
    placed = (
        P(("groups", "pool"), ("ffn", "sub")),
        P(("groups", "pool"), None, ("ffn", "sub")),
        P(("groups", "pool"), None, ("ffn", "sub")),
        P(("groups", "pool"), ("ffn", "sub")),
        P(("groups", "pool"), ("ffn", "sub")),
        P(("groups", "pool")),
        P(("groups", "pool"), ("ffn", "sub")),
        P(("ffn", "sub")),
        P(("ffn", "sub"), "pool"),
        P(("ffn", "sub"), "pool"),
        P("pool", ("ffn", "sub")),
    )
    return jax.shard_map(
        on_device,
        mesh=mesh,
        in_specs=placed,
        out_specs=P(("groups", "pool"), ("ffn", "sub")),
        check_vma=False,
    )
```

profile of v0, /device:TPU:0, one launch (start us, length us, event | category | flops | bytes accessed | tf_op | source)
XLA Modules:
  0.0 142.0 jit_solution(2665024917507169188)
XLA Ops:
  6.5 0.9 iota_compare_fusion
  7.4 0.7 reshape.54
  8.1 0.7 reshape.50
  8.9 1.1 copy.18
  10.0 0.2 fusion.29
  10.2 1.3 fusion.28
  11.5 0.3 fusion.21
  11.9 0.7 fusion.16
  12.6 0.2 copy-done.1
  12.9 0.2 multiply_reduce_fusion
  13.0 8.3 %psum.14 = f32[32]{0:T(128)S(1)} all-reduce(f32[32]{0:T(128)S(1)} %multiply_reduce_fusion), channel_id=1, replica_groups=mesh['groups'=2,'pool'=4,'ffn'=2,'sub'=2] {'ffn','sub'}, use_global_device_ids=true, to_apply=%region_3.4 | all-reduce | flops 32 | bytes 256 | tf_op jit(solution)/shard_map/psum | solution.py:71
  21.4 0.1 multiply_convert_fusion
  21.5 15.5 %all_gather.3 = bf16[128,2048]{1,0:T(8,128)(2,1)S(1)} all-gather(bf16[32,2048]{1,0:T(8,128)(2,1)S(1)} %multiply_convert_fusion), channel_id=1, replica_groups=mesh['groups'=2,'pool'=4,'ffn'=2,'sub'=2] {'pool'}, dimensions={0}, use_global_device_ids=true | all-gather | bytes 655360 | tf_op jit(solution)/shard_map/all_gather | solution.py:76
  37.0 7.3 %convolution_convert_fusion = bf16[128,3584]{1,0:T(8,128)(2,1)S(1)} fusion(bf16[128,2048]{1,0:T(8,128)(2,1)S(1)} %all_gather.3, bf16[2048,3584]{1,0:T(8,128)(2,1)} %param.20), kind=kOutput, calls=%fused_computation | convolution fusion | flops 1879506944 | bytes 16121856 | tf_op jit(solution)/shard_map/dot_general | solution.py:78
  44.3 7.3 %convolution_convert_fusion.1 = bf16[128,3584]{1,0:T(8,128)(2,1)S(1)} fusion(bf16[128,2048]{1,0:T(8,128)(2,1)S(1)} %all_gather.3, bf16[2048,3584]{1,0:T(8,128)(2,1)} %param.19), kind=kOutput, calls=%fused_computation.1 | convolution fusion | flops 1879506944 | bytes 16121856 | tf_op jit(solution)/shard_map/dot_general | solution.py:77
  51.5 1.4 pad_maximum_fusion
  53.0 0.0 all-reduce.2.cloned.1.call-update
  53.0 0.0 reduce-scatter.2.cloned.1.call-start
  53.0 48.4 %all-reduce.2.cloned.1.call-done = bf16[128,7168]{1,0:T(8,128)(2,1)} async-done(((bf16[128,7168]{1,0:T(8,128)(2,1)}), bf16[128,7168]{1,0:T(8,128)(2,1)}) %all-reduce.2.cloned.1.call-update) | async-done | bytes 1835024 | tf_op jit(solution)/shard_map/psum | solution.py:80
  101.4 1.9 %convert_element_type.42 = f32[128,7168]{1,0:T(8,128)S(1)} convert(bf16[128,7168]{1,0:T(8,128)(2,1)} %all-reduce.2.cloned.1.call-done) | non-fusion elementwise | flops 917504 | bytes 5505024 | tf_op jit(solution)/shard_map/convert_element_type | solution.py:80
  103.3 8.3 %convolution_convert_fusion.2 = bf16[128,2048]{1,0:T(8,128)(2,1)} fusion(bf16[3584,2048]{1,0:T(8,128)(2,1)} %param.21, f32[128,7168]{1,0:T(8,128)S(1)} %convert_element_type.42), kind=kOutput, calls=%fused_computation.2 | convolution fusion | flops 1882062848 | bytes 18874368 | tf_op jit(solution)/shard_map/dot_general | solution.py:85
  111.6 0.0 reduce-scatter.2.cloned.1.call-update
  111.6 21.9 %reduce-scatter.2.cloned.1.call-done = bf16[32,2048]{1,0:T(8,128)(2,1)} async-done(((bf16[128,2048]{1,0:T(8,128)(2,1)}), bf16[32,2048]{1,0:T(8,128)(2,1)}) %reduce-scatter.2.cloned.1.call-update) | async-done | bytes 131088 | tf_op jit(solution)/shard_map/reduce_scatter | solution.py:84
  133.4 1.7 %convert_add_fusion = f32[32,2048]{1,0:T(8,128)} fusion(bf16[32,2048]{1,0:T(8,128)(2,1)} %reduce-scatter.2.cloned.1.call-done, f32[32,2048]{1,0:T(8,128)S(1)} %copy-done.1, f32[4,8,16,128]{3,2,1,0:T(8,128)S(1)} %bitcast.49), kind=kLoop, calls=%fused_computation.18 | loop fusion | flops 196608 | bytes 917504 | tf_op jit(solution)/shard_map/add | solution.py:90
  (12 shorter events, 0.1 us)
Async XLA Ops:
  6.5 3.6 %copy-start = (bf16[32,128,256]{2,1,0:T(8,128)(2,1)S(1)}, bf16[32,128,256]{2,1,0:T(8,128)(2,1)}, u32[]{:S(2)}) copy-start(bf16[32,128,256]{2,1,0:T(8,128)(2,1)} %param.12) | copy-start | bytes 6291460
  6.5 94.9 %all-reduce.2.cloned.1.call-start = ((), (), s32[]{:S(2)}) async-start(), calls=%async_computation.1 | async-start | bytes 3670016 | tf_op jit(solution)/shard_map/psum | solution.py:80
  8.9 3.0 %copy-start.3 = (bf16[32,128,256]{2,1,0:T(8,128)(2,1)S(1)}, bf16[32,128,256]{2,1,0:T(8,128)(2,1)}, u32[]{:S(2)}) copy-start(bf16[32,128,256]{2,1,0:T(8,128)(2,1)} %param.13) | copy-start | bytes 6291460
  11.9 1.0 copy-start.1
  11.9 9.5 %copy-start.2 = (f32[2048]{0:T(1024)S(1)}, f32[2048]{0:T(1024)}, u32[]{:S(2)}) copy-start(f32[2048]{0:T(1024)} %param.18) | copy-start | bytes 24580
  53.0 80.5 %reduce-scatter.2.cloned.1.call-start = ((), (), s32[]{:S(2)}) async-start(), calls=%async_computation.2 | async-start | bytes 655360 | tf_op jit(solution)/shard_map/reduce_scatter | solution.py:84
Sparse Core Ops, SparseCore 0:
  53.1 48.2 all-reduce.1
  111.7 21.6 reduce-scatter.1
where the time goes:
time: 142 us
  waiting for transfers between devices  70.3 us (50%)
  matrix products  25 us (18%)
  blocking collectives  23.8 us (17%)
  between operations  13.5 us (10%)
  other arithmetic  6.52 us (5%)
  local copies, waits for them, and re-layouts  2.77 us (2%)
    psum x1, waiting for transfers between devices, layer_rows(): lax.psum(partial_value.astype(jnp.bfloat16), ('ffn', 'sub'))  48.4 us
    reduce_scatter x1, waiting for transfers between devices, layer_rows(): lax.psum_scatter(jnp.dot(hidden_units, down_weight, preferred_element_typ...  21.9 us
    all_gather x1, blocking collectives, layer_rows(): block_rows = lax.all_gather(normed, 'pool', axis=0, tiled=True)  15.5 us
    psum x1, blocking collectives, layer_rows(): lax.psum(jnp.sum(hidden_state * hidden_state, axis=1), ('ffn', 'sub'))  8.33 us
    dot_general x1, matrix products, layer_rows(): jnp.dot(hidden_units, down_weight, preferred_element_type=jnp.float32)  8.27 us
    dot_general x1, matrix products, layer_rows(): jnp.dot(block_rows, gate_weight, preferred_element_type=jnp.float32)  7.27 us
    dot_general x1, matrix products, layer_rows(): up_part = jnp.dot(block_rows, up_weight, preferred_element_type=jnp.float32)  7.27 us
  transfers between devices with their start and end apart: 2, of which 2 were waited for; matrix products, arithmetic and copies ran while one was open for 0% of the time, Pallas kernels for 0%

commit v1 on v0

--- a/solution.py
+++ b/solution.py
@@ -1,12 +1,17 @@
+import functools
 import math
 
 import jax
 import jax.numpy as jnp
 from jax import lax
+from jax.experimental import pallas as pl
+from jax.experimental.pallas import tpu as pltpu
 from jax.sharding import PartitionSpec as P
 
 HEAD_DIM = 128
 D = 8192
+MESH = pl.DeviceIdType.MESH
+VMEM_BYTES = 60 * 1024 * 1024
 
 
 def rounded(values):
@@ -90,32 +95,348 @@
     return hidden_state + ffn_total
 
 
-def on_device(
-    queries,
-    cache_keys,
-    cache_values,
-    new_keys,
-    new_values,
-    kv_lengths,
-    residual,
-    norm_gain,
-    gate_weight,
-    up_weight,
-    down_weight,
+def fused_kernel(
+    n_pool,
+    q_hbm, k_hbm, v_hbm, nk_ref, nv_ref, len_ref, res_hbm, gain_ref, g_hbm, u_hbm, d_hbm,
+    out_ref,
+    qbuf, kbuf, vbuf, res, gw, uw, dw,
+    qs, nkx, nvx, att, hid, xall, sqp, sqall,
+    s1, r1, s2, r2, s3, r3, hall, acc, dsend, drecv,
+    in_sem, w_sem, xs_sem, xr_sem, qs_sem, qr_sem, ts_sem, tr_sem,
+    ps_sem, pr_sem, hs_sem, hr_sem, ds_sem, dr_sem,
 ):
-    return layer_rows(
-        queries,
-        cache_keys,
-        cache_values,
-        new_keys,
-        new_values,
-        kv_lengths,
-        residual,
-        norm_gain,
-        gate_weight,
-        up_weight,
-        down_weight,
-    )
+    rows, width = qbuf.shape
+    cap_len = kbuf.shape[1]
+    kv_local = kbuf.shape[2] // HEAD_DIM
+    heads = width // HEAD_DIM
+    group_size = heads // kv_local
+    units = hall.shape[2]
+    half = rows // 2
+    scaling = 1.0 / math.sqrt(HEAD_DIM)
+    f32, bf16 = jnp.float32, jnp.bfloat16
+
+    p = lax.axis_index("pool")
+    f = lax.axis_index("ffn")
+    s = lax.axis_index("sub")
+    me = f * 2 + s
+    pool_at = [lax.rem(p + d, n_pool) for d in range(1, n_pool)]
+    sibling = {"sub": 1 - s}
+    across = {"ffn": 1 - f}
+    diagonal = {"ffn": 1 - f, "sub": 1 - s}
+    near = [sibling, across, diagonal]
+
+    def remote(src, dst, send, recv, to):
+        return pltpu.make_async_remote_copy(
+            src_ref=src, dst_ref=dst, send_sem=send, recv_sem=recv,
+            device_id=to, device_id_type=MESH,
+        )
+
+    early = [
+        pltpu.make_async_copy(q_hbm, qbuf, in_sem.at[0]),
+        pltpu.make_async_copy(res_hbm, res, in_sem.at[1]),
+    ]
+    caches = []
+    for c in range(2):
+        at = pl.ds(c * half, half)
+        caches.append(
+            [
+                pltpu.make_async_copy(k_hbm.at[at], kbuf.at[at], in_sem.at[2 + 2 * c]),
+                pltpu.make_async_copy(v_hbm.at[at], vbuf.at[at], in_sem.at[3 + 2 * c]),
+            ]
+        )
+    for copy in early + caches[0] + caches[1]:
+        copy.start()
+    weights = []
+    for i, (src, dst) in enumerate(((g_hbm, gw), (u_hbm, uw), (d_hbm, dw))):
+        step = src.shape[0] // 4
+        weights.append(
+            [
+                pltpu.make_async_copy(
+                    src.at[pl.ds(t * step, step)], dst.at[pl.ds(t * step, step)], w_sem.at[i, t]
+                )
+                for t in range(4)
+            ]
+        )
+
+    barrier = pltpu.get_barrier_semaphore()
+    for to in near + [{"pool": t} for t in pool_at]:
+        pl.semaphore_signal(barrier, inc=1, device_id=to, device_id_type=MESH)
+
+    for copy in early:
+        copy.wait()
+    for h in range(heads):
+        kv = h // group_size
+        qs[:, h, :] = qbuf[:, h * HEAD_DIM : (h + 1) * HEAD_DIM].astype(f32)
+        nkx[:, h, :] = nk_ref[:, kv * HEAD_DIM : (kv + 1) * HEAD_DIM].astype(f32)
+        nvx[:, h, :] = nv_ref[:, kv * HEAD_DIM : (kv + 1) * HEAD_DIM].astype(f32)
+
+    batch = 8
+    head_row = lax.broadcasted_iota(jnp.int32, (heads, HEAD_DIM), 0) // group_size
+    lane = lax.broadcasted_iota(jnp.int32, (heads, cap_len), 1)
+
+    def attend_batch(first):
+        q3 = qs[pl.ds(first, batch)]
+        self_score = jnp.sum(q3 * nkx[pl.ds(first, batch)], axis=2, keepdims=True) * scaling
+        scores = []
+        for b in range(batch):
+            q = q3[b].astype(bf16)
+            zero = jnp.zeros_like(q)
+            wide = jnp.concatenate(
+                [jnp.where(head_row == kv, q, zero) for kv in range(kv_local)], axis=1
+            )
+            raw = lax.dot_general(
+                wide, kbuf[first + b], (((1,), (1,)), ((), ())), preferred_element_type=f32
+            )
+            scores.append(jnp.where(lane < len_ref[first + b], raw * scaling, -jnp.inf))
+        scores = jnp.stack(scores)
+        largest = jnp.maximum(jnp.max(scores, axis=2, keepdims=True), self_score)
+        expo = jnp.exp(scores - largest)
+        self_expo = jnp.exp(self_score - largest)
+        totals = jnp.sum(expo, axis=2, keepdims=True) + self_expo
+        weight = expo.astype(bf16)
+        self_weight = self_expo.astype(bf16).astype(f32)
+        mixed = []
+        for b in range(batch):
+            wide = jnp.dot(weight[b], vbuf[first + b], preferred_element_type=f32)
+            one = wide[:, :HEAD_DIM]
+            for kv in range(1, kv_local):
+                one = jnp.where(
+                    head_row == kv, wide[:, kv * HEAD_DIM : (kv + 1) * HEAD_DIM], one
+                )
+            mixed.append(one)
+        mixed = jnp.stack(mixed) + self_weight * nvx[pl.ds(first, batch)]
+        att[pl.ds(first, batch)] = mixed / totals
+
+    gathers = []
+    for c in range(2):
+        for copy in caches[c]:
+            copy.wait()
+        for copy in weights[c]:
+            copy.start()
+
+        @pl.loop(0, half // batch)
+        def _(i):
+            attend_batch(c * half + i * batch)
+
+        at = pl.ds(c * half, half)
+        mine = pl.ds(pl.multiple_of(p * rows + c * half, half), half)
+        squares = jnp.zeros((half, HEAD_DIM), f32)
+        for h in range(heads):
+            cols = pl.ds(h * HEAD_DIM, HEAD_DIM)
+            state = res[at, cols] + att[at, h, :]
+            hid[at, cols] = state
+            squares = squares + state * state
+            xall[mine, cols] = (state * gain_ref[:, cols]).astype(bf16)
+        sqp[me, at] = jnp.broadcast_to(
+            jnp.sum(squares, axis=1, keepdims=True), (half, HEAD_DIM)
+        )
+        if c == 0:
+            pl.semaphore_wait(barrier, 3 + n_pool - 1)
+        for d, to in enumerate(pool_at):
+            copy = remote(
+                xall.at[mine], xall.at[mine], xs_sem.at[c, d], xr_sem.at[c, d], {"pool": to}
+            )
+            copy.start()
+            gathers.append(copy)
+    for copy in weights[2]:
+        copy.start()
+
+    parts_sent = [
+        remote(sqp.at[me], sqp.at[me], qs_sem.at[i], qr_sem.at[i], to)
+        for i, to in enumerate(near)
+    ]
+    for copy in parts_sent:
+        copy.start()
+    for copy in parts_sent:
+        copy.wait()
+    sqall[p] = sqp[0] + sqp[1] + sqp[2] + sqp[3]
+    sums_sent = [
+        remote(sqall.at[p], sqall.at[p], ts_sem.at[d], tr_sem.at[d], {"pool": to})
+        for d, to in enumerate(pool_at)
+    ]
+    for copy in sums_sent:
+        copy.start()
+
+    for w in weights[:2]:
+        for copy in w:
+            copy.wait()
+    for copy in gathers:
+        copy.wait()
+
+    def part(w, j):
+        return jnp.dot(
+            xall[...],
+            w[:, pl.ds(pl.multiple_of(j * units, HEAD_DIM), units)],
+            preferred_element_type=f32,
+        )
+
+    held = []
+    pair = (gw, uw)
+    for c in range(2):
+        s1[c] = part(pair[c], 3 - me).astype(bf16)
+        first = remote(s1.at[c], r1.at[c], ps_sem.at[0, c], pr_sem.at[0, c], sibling)
+        first.start()
+        value = part(pair[c], (1 - f) * 2 + s)
+        first.wait()
+        s2[c] = (value.astype(bf16).astype(f32) + r1[c].astype(f32)).astype(bf16)
+        second = remote(s2.at[c], r2.at[c], ps_sem.at[1, c], pr_sem.at[1, c], across)
+        second.start()
+        held.append(second)
+    for c in range(2):
+        s3[c] = part(pair[c], f * 2 + 1 - s).astype(bf16)
+        third = remote(s3.at[c], r3.at[c], ps_sem.at[2, c], pr_sem.at[2, c], sibling)
+        third.start()
+        held.append(third)
+    own = [part(pair[c], me) for c in range(2)]
+    for copy in sums_sent:
+        copy.wait()
+    scale = lax.rsqrt(sqall[...].reshape(n_pool * rows, HEAD_DIM)[:, :1] / D + 1e-05)
+    for copy in held:
+        copy.wait()
+    gate, up = [
+        (own[c].astype(bf16).astype(f32) + r3[c].astype(f32) + r2[c].astype(f32)) * scale
+        for c in range(2)
+    ]
+    hall[me] = (gate / (1.0 + jnp.exp(-gate)) * up).astype(bf16)
+
+    to_across = remote(hall.at[me], hall.at[me], hs_sem.at[0], hr_sem.at[0], across)
+    to_sibling = remote(hall.at[me], hall.at[me], hs_sem.at[1], hr_sem.at[1], sibling)
+    to_across.start()
+    to_sibling.start()
+    for copy in weights[2]:
+        copy.wait()
+    tile = 512
+
+    def down(j, cols):
+        return jnp.dot(
+            hall[j],
+            dw[pl.ds(pl.multiple_of(j * units, HEAD_DIM), units), cols],
+            preferred_element_type=f32,
+        )
+
+    def column(i):
+        return pl.ds(pl.multiple_of(i * tile, tile), tile)
+
+    @pl.loop(0, width // tile)
+    def _(i):
+        acc[:, column(i)] = down(me, column(i))
+
+    to_sibling.wait()
+
+    @pl.loop(0, width // tile)
+    def _(i):
+        acc[:, column(i)] += down(f * 2 + 1 - s, column(i))
+
+    to_across.wait()
+    other = (1 - f) * 2 + s
+    passed = remote(hall.at[other], hall.at[other], hs_sem.at[2], hr_sem.at[2], sibling)
+    passed.start()
+
+    @pl.loop(0, width // tile)
+    def _(i):
+        acc[:, column(i)] += down(other, column(i))
+
+    passed.wait()
+    scattered = []
+    pieces = width // tile
+    for i in range(pieces):
+        cols = pl.ds(i * tile, tile)
+        dsend[:, cols] = (acc[:, cols] + down(3 - me, cols)).astype(bf16)
+        for d, to in enumerate(pool_at):
+            copy = remote(
+                dsend.at[pl.ds(pl.multiple_of(to * rows, rows), rows), cols],
+                drecv.at[p, :, cols],
+                ds_sem.at[i, d], dr_sem.at[i, d], {"pool": to},
+            )
+            copy.start()
+            scattered.append(copy)
+    drecv[p] = dsend[pl.ds(pl.multiple_of(p * rows, rows), rows), :]
+    for i in range(pieces):
+        cols = pl.ds(i * tile, tile)
+        for copy in scattered[i * (n_pool - 1) : (i + 1) * (n_pool - 1)]:
+            copy.wait()
+        total = drecv[0, :, cols].astype(f32)
+        for k in range(1, n_pool):
+            total = total + drecv[k, :, cols].astype(f32)
+        out_ref[:, cols] = hid[:, cols] + total
+
+
+def fused_rows(
+    n_pool, queries, cache_keys, cache_values, new_keys, new_values, kv_lengths,
+    residual, norm_gain, gate_weight, up_weight, down_weight,
+):
+    rows, width = queries.shape
+    every = n_pool * rows
+    unit_width = gate_weight.shape[1]
+    units = unit_width // 4
+    heads = width // HEAD_DIM
+    f32, bf16 = jnp.float32, jnp.bfloat16
+    anywhere = pl.BlockSpec(memory_space=pl.ANY)
+    vmem = pl.BlockSpec(memory_space=pltpu.VMEM)
+    smem = pl.BlockSpec(memory_space=pltpu.SMEM)
+    per_head = pltpu.VMEM((rows, heads, HEAD_DIM), f32)
+    pair = pltpu.VMEM((2, every, units), bf16)
+    dma = pltpu.SemaphoreType.DMA
+    far = n_pool - 1
+    return pl.pallas_call(
+        functools.partial(fused_kernel, n_pool),
+        out_shape=jax.ShapeDtypeStruct((rows, width), f32),
+        in_specs=[anywhere] * 3 + [vmem] * 2 + [smem, anywhere, vmem] + [anywhere] * 3,
+        out_specs=vmem,
+        scratch_shapes=[
+            pltpu.VMEM(queries.shape, bf16),
+            pltpu.VMEM(cache_keys.shape, bf16),
+            pltpu.VMEM(cache_values.shape, bf16),
+            pltpu.VMEM(residual.shape, f32),
+            pltpu.VMEM(gate_weight.shape, bf16),
+            pltpu.VMEM(up_weight.shape, bf16),
+            pltpu.VMEM(down_weight.shape, bf16),
+            per_head, per_head, per_head, per_head,
+            pltpu.VMEM((rows, width), f32),
+            pltpu.VMEM((every, width), bf16),
+            pltpu.VMEM((4, rows, HEAD_DIM), f32),
+            pltpu.VMEM((n_pool, rows, HEAD_DIM), f32),
+            pair, pair, pair, pair, pair, pair,
+            pltpu.VMEM((4, every, units), bf16),
+            pltpu.VMEM((every, width), f32),
+            pltpu.VMEM((every, width), bf16),
+            pltpu.VMEM((n_pool, rows, width), bf16),
+            dma((6,)), dma((3, 4)),
+            dma((2, far)), dma((2, far)), dma((3,)), dma((3,)), dma((far,)), dma((far,)),
+            dma((3, 2)), dma((3, 2)), dma((3,)), dma((3,)),
+            dma((width // 512, far)), dma((width // 512, far)),
+        ],
+        compiler_params=pltpu.CompilerParams(
+            collective_id=0, has_side_effects=True, vmem_limit_bytes=VMEM_BYTES
+        ),
+    )(
+        queries, cache_keys, cache_values, new_keys, new_values, kv_lengths, residual,
+        norm_gain.reshape(1, width), gate_weight, up_weight, down_weight,
+    )
+
+
+def fits(n_pool, n_ffn, n_sub, queries, cache_keys, gate_weight, down_weight):
+    rows, width = queries.shape
+    unit_width = gate_weight.shape[1]
+    weight_bytes = 2 * (2 * gate_weight.size + down_weight.size)
+    return (
+        n_ffn == 2
+        and n_sub == 2
+        and n_pool > 1
+        and rows % 32 == 0
+        and width % 512 == 0
+        and unit_width % (4 * HEAD_DIM) == 0
+        and weight_bytes + 4 * cache_keys.size + 24 * n_pool * rows * unit_width
+        <= VMEM_BYTES
+    )
+
+
+def on_device(mesh_shape, *operands):
+    n_pool, n_ffn, n_sub = mesh_shape["pool"], mesh_shape["ffn"], mesh_shape["sub"]
+    queries, cache_keys = operands[0], operands[1]
+    if fits(n_pool, n_ffn, n_sub, queries, cache_keys, operands[8], operands[10]):
+        return fused_rows(n_pool, *operands)
+    return layer_rows(*operands)
 
 
 def solution(mesh):
@@ -133,7 +454,7 @@
         P("pool", ("ffn", "sub")),
     )
     return jax.shard_map(
-        on_device,
+        functools.partial(on_device, dict(mesh.shape)),
         mesh=mesh,
         in_specs=placed,
         out_specs=P(("groups", "pool"), ("ffn", "sub")),

time: 142 us -> 58.1 us (0.41)
  waiting for transfers between devices: 70.3 us -> 0 us
  Pallas kernels: 0 us -> 56.2 us
  matrix products: 25 us -> 0 us
  blocking collectives: 23.8 us -> 0 us
  between operations: 13.5 us -> 0.01 us
  other arithmetic: 6.52 us -> 0 us
    pallas_call x0 -> x1, Pallas kernels: none -> 56.2 us  [fused_rows(): pl.pallas_call(functools.partial(fused_kernel, n_pool), out_shape=jax.Sha...]
    psum x1 -> x0, waiting for transfers between devices: 48.4 us -> none  [layer_rows(): lax.psum(partial_value.astype(jnp.bfloat16), ('ffn', 'sub'))]
    dot_general x6 -> x0, matrix products: 25 us -> none  [the longest x1 8.27 us: layer_rows(): jnp.dot(hidden_units, down_weight, preferred_element_type=jnp.float32)]
    reduce_scatter x1 -> x0, waiting for transfers between devices: 21.9 us -> none  [layer_rows(): lax.psum_scatter(jnp.dot(hidden_units, down_weight, preferred_element_typ...]
    all_gather x1 -> x0, blocking collectives: 15.5 us -> none  [layer_rows(): block_rows = lax.all_gather(normed, 'pool', axis=0, tiled=True)]
    psum x1 -> x0, blocking collectives: 8.33 us -> none  [layer_rows(): lax.psum(jnp.sum(hidden_state * hidden_state, axis=1), ('ffn', 'sub'))]
    convert_element_type x4 -> x0, other arithmetic: 2.02 us -> none  [the longest x1 1.85 us: layer_rows(): lax.psum(partial_value.astype(jnp.bfloat16), ('ffn', 'sub'))]
    add x1 -> x0, other arithmetic: 1.71 us -> none  [layer_rows(): return hidden_state + ffn_total]
  transfers between devices with their start and end apart: 2 -> 0, of which waited for: 2 -> 0; matrix products, arithmetic and copies ran while one was open for 0% -> 0% of each run, Pallas kernels for 0% -> 0%
where the time goes in v1:
time: 58.1 us; the launch traced here: 57.8 us
  Pallas kernels  56.2 us (97%)
  local copies, waits for them, and re-layouts  1.67 us (3%)
    pallas_call x1, Pallas kernels, fused_rows(): pl.pallas_call(functools.partial(fused_kernel, n_pool), out_shape=jax.Sha...  56.2 us
    unnamed x1, local copies, waits for them, and re-layouts  1.67 us

profile of v1, /device:TPU:0, one launch (start us, length us, event | category | flops | bytes accessed | tf_op | source)
XLA Modules:
  0.0 57.8 jit_solution(15139845629290200086)
XLA Ops:
  0.0 56.2 %shard_map.109 = f32[32,2048]{1,0:T(8,128)} custom-call(bf16[32,2048]{1,0:T(8,128)(2,1)} %q_hbm.1, bf16[32,128,256]{2,1,0:T(8,128)(2,1)} %k_hbm.1, bf16[32,128,256]{2,1,0:T(8,128)(2,1)} %v_hbm.1, bf16[32,256]{1,0:T(8,128)(2,1)} %nk_ref.1, bf16[32,256]{1,0:T(8,128)(2,1)} %nv_ref.1, s32[32]{0:T(128)} %len_ref.1, f32[32,2048]{1,0:T(8,128)} %res_hbm.1, ...), custom_call_target="tpu_custom_call" | custom-call | tf_op jit(solution)/shard_map/pallas_call | solution.py:381
  56.2 1.7 %copy.13 = f32[32,2048]{1,0:T(8,128)} copy(f32[32,2048]{1,0:T(8,128)} %shard_map.109) | data formatting | bytes 524288

commit v2 on v1

--- a/solution.py
+++ b/solution.py
@@ -101,7 +101,7 @@
     out_ref,
     qbuf, kbuf, vbuf, res, gw, uw, dw,
     qs, nkx, nvx, att, hid, xall, sqp, sqall,
-    s1, r1, s2, r2, s3, r3, hall, acc, dsend, drecv,
+    s1, r1, s2, r2, s3, r3, own, hall, acc, dsend, drecv,
     in_sem, w_sem, xs_sem, xr_sem, qs_sem, qr_sem, ts_sem, tr_sem,
     ps_sem, pr_sem, hs_sem, hr_sem, ds_sem, dr_sem,
 ):
@@ -110,7 +110,7 @@
     kv_local = kbuf.shape[2] // HEAD_DIM
     heads = width // HEAD_DIM
     group_size = heads // kv_local
-    units = hall.shape[2]
+    units = hall.shape[3]
     half = rows // 2
     scaling = 1.0 / math.sqrt(HEAD_DIM)
     f32, bf16 = jnp.float32, jnp.bfloat16
@@ -207,7 +207,7 @@
         mixed = jnp.stack(mixed) + self_weight * nvx[pl.ds(first, batch)]
         att[pl.ds(first, batch)] = mixed / totals
 
-    gathers = []
+    gathers, started = ([], []), []
     for c in range(2):
         for copy in caches[c]:
             copy.wait()
@@ -219,14 +219,14 @@
             attend_batch(c * half + i * batch)
 
         at = pl.ds(c * half, half)
-        mine = pl.ds(pl.multiple_of(p * rows + c * half, half), half)
+        mine = pl.ds(pl.multiple_of(p * half, half), half)
         squares = jnp.zeros((half, HEAD_DIM), f32)
         for h in range(heads):
             cols = pl.ds(h * HEAD_DIM, HEAD_DIM)
             state = res[at, cols] + att[at, h, :]
             hid[at, cols] = state
             squares = squares + state * state
-            xall[mine, cols] = (state * gain_ref[:, cols]).astype(bf16)
+            xall[c, mine, cols] = (state * gain_ref[:, cols]).astype(bf16)
         sqp[me, at] = jnp.broadcast_to(
             jnp.sum(squares, axis=1, keepdims=True), (half, HEAD_DIM)
         )
@@ -234,10 +234,11 @@
             pl.semaphore_wait(barrier, 3 + n_pool - 1)
         for d, to in enumerate(pool_at):
             copy = remote(
-                xall.at[mine], xall.at[mine], xs_sem.at[c, d], xr_sem.at[c, d], {"pool": to}
+                xall.at[c, mine], xall.at[c, mine], xs_sem.at[c, d], xr_sem.at[c, d], {"pool": to}
             )
             copy.start()
-            gathers.append(copy)
+            gathers[c].append(copy)
+            started.append(copy)
     for copy in weights[2]:
         copy.start()
 
@@ -247,69 +248,80 @@
     ]
     for copy in parts_sent:
         copy.start()
-    for copy in parts_sent:
-        copy.wait()
-    sqall[p] = sqp[0] + sqp[1] + sqp[2] + sqp[3]
+    started.extend(parts_sent)
     sums_sent = [
         remote(sqall.at[p], sqall.at[p], ts_sem.at[d], tr_sem.at[d], {"pool": to})
         for d, to in enumerate(pool_at)
     ]
-    for copy in sums_sent:
-        copy.start()
-
-    for w in weights[:2]:
-        for copy in w:
-            copy.wait()
-    for copy in gathers:
-        copy.wait()
-
-    def part(w, j):
+    started.extend(sums_sent)
+
+    def spread_squares():
+        for copy in parts_sent:
+            copy.wait_recv()
+        sqall[p] = sqp[0] + sqp[1] + sqp[2] + sqp[3]
+        for copy in sums_sent:
+            copy.start()
+
+    pair = (gw, uw)
+    sibling_unit, across_unit, diagonal_unit = f * 2 + 1 - s, (1 - f) * 2 + s, 3 - me
+    awaited = ([], [])
+
+    def part(c, w, j):
         return jnp.dot(
-            xall[...],
-            w[:, pl.ds(pl.multiple_of(j * units, HEAD_DIM), units)],
+            xall[c],
+            pair[w][:, pl.ds(pl.multiple_of(j * units, HEAD_DIM), units)],
             preferred_element_type=f32,
         )
 
-    held = []
-    pair = (gw, uw)
-    for c in range(2):
-        s1[c] = part(pair[c], 3 - me).astype(bf16)
-        first = remote(s1.at[c], r1.at[c], ps_sem.at[0, c], pr_sem.at[0, c], sibling)
+    def reduce_out(c, w):
+        s1[c, w] = part(c, w, diagonal_unit).astype(bf16)
+        first = remote(s1.at[c, w], r1.at[c, w], ps_sem.at[c, 0, w], pr_sem.at[c, 0, w], sibling)
         first.start()
-        value = part(pair[c], (1 - f) * 2 + s)
-        first.wait()
-        s2[c] = (value.astype(bf16).astype(f32) + r1[c].astype(f32)).astype(bf16)
-        second = remote(s2.at[c], r2.at[c], ps_sem.at[1, c], pr_sem.at[1, c], across)
+        value = part(c, w, across_unit)
+        first.wait_recv()
+        s2[c, w] = (value.astype(bf16).astype(f32) + r1[c, w].astype(f32)).astype(bf16)
+        second = remote(s2.at[c, w], r2.at[c, w], ps_sem.at[c, 1, w], pr_sem.at[c, 1, w], across)
         second.start()
-        held.append(second)
-    for c in range(2):
-        s3[c] = part(pair[c], f * 2 + 1 - s).astype(bf16)
-        third = remote(s3.at[c], r3.at[c], ps_sem.at[2, c], pr_sem.at[2, c], sibling)
-        third.start()
-        held.append(third)
-    own = [part(pair[c], me) for c in range(2)]
-    for copy in sums_sent:
-        copy.wait()
-    scale = lax.rsqrt(sqall[...].reshape(n_pool * rows, HEAD_DIM)[:, :1] / D + 1e-05)
-    for copy in held:
-        copy.wait()
-    gate, up = [
-        (own[c].astype(bf16).astype(f32) + r3[c].astype(f32) + r2[c].astype(f32)) * scale
-        for c in range(2)
-    ]
-    hall[me] = (gate / (1.0 + jnp.exp(-gate)) * up).astype(bf16)
-
-    to_across = remote(hall.at[me], hall.at[me], hs_sem.at[0], hr_sem.at[0], across)
-    to_sibling = remote(hall.at[me], hall.at[me], hs_sem.at[1], hr_sem.at[1], sibling)
-    to_across.start()
-    to_sibling.start()
-    for copy in weights[2]:
-        copy.wait()
+        started.extend([first, second])
+        awaited[c].append(second)
+
+    def reduce_in(c):
+        for w in range(2):
+            s3[c, w] = part(c, w, sibling_unit).astype(bf16)
+            third = remote(
+                s3.at[c, w], r3.at[c, w], ps_sem.at[c, 2, w], pr_sem.at[c, 2, w], sibling
+            )
+            third.start()
+            started.append(third)
+            awaited[c].append(third)
+            own[c, w] = part(c, w, me).astype(bf16)
+
+    def activate(c):
+        squares = sqall[:, c * half : (c + 1) * half, :].reshape(n_pool * half, HEAD_DIM)
+        scale = lax.rsqrt(squares[:, :1] / D + 1e-05)
+        for copy in awaited[c]:
+            copy.wait_recv()
+        gate, up = [
+            (own[c, w].astype(f32) + r3[c, w].astype(f32) + r2[c, w].astype(f32)) * scale
+            for w in range(2)
+        ]
+        hall[c, me] = (gate / (1.0 + jnp.exp(-gate)) * up).astype(bf16)
+        mine = hall.at[c, me]
+        to_across = remote(mine, mine, hs_sem.at[c, 0], hr_sem.at[c, 0], across)
+        to_sibling = remote(mine, mine, hs_sem.at[c, 1], hr_sem.at[c, 1], sibling)
+        to_across.start()
+        to_sibling.start()
+        started.extend([to_across, to_sibling])
+        return to_across, to_sibling
+
     tile = 512
-
-    def down(j, cols):
+    pieces = 2
+    piece = width // pieces
+    scattered = ([], [])
+
+    def down(c, j, cols):
         return jnp.dot(
-            hall[j],
+            hall[c, j],
             dw[pl.ds(pl.multiple_of(j * units, HEAD_DIM), units), cols],
             preferred_element_type=f32,
         )
@@ -317,48 +329,89 @@
     def column(i):
         return pl.ds(pl.multiple_of(i * tile, tile), tile)
 
-    @pl.loop(0, width // tile)
-    def _(i):
-        acc[:, column(i)] = down(me, column(i))
-
-    to_sibling.wait()
-
-    @pl.loop(0, width // tile)
-    def _(i):
-        acc[:, column(i)] += down(f * 2 + 1 - s, column(i))
-
-    to_across.wait()
-    other = (1 - f) * 2 + s
-    passed = remote(hall.at[other], hall.at[other], hs_sem.at[2], hr_sem.at[2], sibling)
-    passed.start()
-
-    @pl.loop(0, width // tile)
-    def _(i):
-        acc[:, column(i)] += down(other, column(i))
-
-    passed.wait()
-    scattered = []
-    pieces = width // tile
-    for i in range(pieces):
-        cols = pl.ds(i * tile, tile)
-        dsend[:, cols] = (acc[:, cols] + down(3 - me, cols)).astype(bf16)
-        for d, to in enumerate(pool_at):
-            copy = remote(
-                dsend.at[pl.ds(pl.multiple_of(to * rows, rows), rows), cols],
-                drecv.at[p, :, cols],
-                ds_sem.at[i, d], dr_sem.at[i, d], {"pool": to},
-            )
-            copy.start()
-            scattered.append(copy)
-    drecv[p] = dsend[pl.ds(pl.multiple_of(p * rows, rows), rows), :]
-    for i in range(pieces):
-        cols = pl.ds(i * tile, tile)
-        for copy in scattered[i * (n_pool - 1) : (i + 1) * (n_pool - 1)]:
+    def project(c, to_across, to_sibling):
+        @pl.loop(0, width // tile)
+        def _(i):
+            acc[:, column(i)] = down(c, me, column(i))
+
+        to_sibling.wait_recv()
+
+        @pl.loop(0, width // tile)
+        def _(i):
+            acc[:, column(i)] += down(c, sibling_unit, column(i))
+
+        to_across.wait_recv()
+        held = hall.at[c, across_unit]
+        passed = remote(held, held, hs_sem.at[c, 2], hr_sem.at[c, 2], sibling)
+        passed.start()
+        started.append(passed)
+
+        @pl.loop(0, width // tile)
+        def _(i):
+            acc[:, column(i)] += down(c, across_unit, column(i))
+
+        passed.wait_recv()
+        for i in range(pieces):
+
+            @pl.loop(i * piece // tile, (i + 1) * piece // tile)
+            def _(t):
+                dsend[c, :, column(t)] = (
+                    acc[:, column(t)] + down(c, diagonal_unit, column(t))
+                ).astype(bf16)
+
+            cols = pl.ds(i * piece, piece)
+            for d, to in enumerate(pool_at):
+                copy = remote(
+                    dsend.at[c, pl.ds(pl.multiple_of(to * half, half), half), cols],
+                    drecv.at[c, p, :, cols],
+                    ds_sem.at[c, i, d], dr_sem.at[c, i, d], {"pool": to},
+                )
+                copy.start()
+                scattered[c].append(copy)
+                started.append(copy)
+        drecv[c, p] = dsend[c, pl.ds(pl.multiple_of(p * half, half), half), :]
+
+    def collect(c):
+        at = pl.ds(c * half, half)
+        far = n_pool - 1
+        for i in range(pieces):
+            cols = pl.ds(i * piece, piece)
+            for copy in scattered[c][i * far : (i + 1) * far]:
+                copy.wait_recv()
+            total = drecv[c, 0, :, cols].astype(f32)
+            for k in range(1, n_pool):
+                total = total + drecv[c, k, :, cols].astype(f32)
+            out_ref[at, cols] = hid[at, cols] + total
+
+    def ready(copies):
+        for copy in copies:
             copy.wait()
-        total = drecv[0, :, cols].astype(f32)
-        for k in range(1, n_pool):
-            total = total + drecv[k, :, cols].astype(f32)
-        out_ref[:, cols] = hid[:, cols] + total
+
+    def arrived(copies):
+        for copy in copies:
+            copy.wait_recv()
+
+    ready(weights[0])
+    arrived(gathers[0])
+    reduce_out(0, 0)
+    spread_squares()
+    ready(weights[1])
+    reduce_out(0, 1)
+    reduce_in(0)
+    arrived(gathers[1])
+    reduce_out(1, 0)
+    arrived(sums_sent)
+    sent = activate(0)
+    reduce_out(1, 1)
+    reduce_in(1)
+    ready(weights[2])
+    project(0, *sent)
+    sent = activate(1)
+    project(1, *sent)
+    collect(0)
+    collect(1)
+    for copy in started:
+        copy.wait_send()
 
 
 def fused_rows(
@@ -375,7 +428,7 @@
     vmem = pl.BlockSpec(memory_space=pltpu.VMEM)
     smem = pl.BlockSpec(memory_space=pltpu.SMEM)
     per_head = pltpu.VMEM((rows, heads, HEAD_DIM), f32)
-    pair = pltpu.VMEM((2, every, units), bf16)
+    pair = pltpu.VMEM((2, 2, every // 2, units), bf16)
     dma = pltpu.SemaphoreType.DMA
     far = n_pool - 1
     return pl.pallas_call(
@@ -393,18 +446,18 @@
             pltpu.VMEM(down_weight.shape, bf16),
             per_head, per_head, per_head, per_head,
             pltpu.VMEM((rows, width), f32),
-            pltpu.VMEM((every, width), bf16),
+            pltpu.VMEM((2, every // 2, width), bf16),
             pltpu.VMEM((4, rows, HEAD_DIM), f32),
             pltpu.VMEM((n_pool, rows, HEAD_DIM), f32),
-            pair, pair, pair, pair, pair, pair,
-            pltpu.VMEM((4, every, units), bf16),
-            pltpu.VMEM((every, width), f32),
-            pltpu.VMEM((every, width), bf16),
-            pltpu.VMEM((n_pool, rows, width), bf16),
+            pair, pair, pair, pair, pair, pair, pair,
+            pltpu.VMEM((2, 4, every // 2, units), bf16),
+            pltpu.VMEM((every // 2, width), f32),
+            pltpu.VMEM((2, every // 2, width), bf16),
+            pltpu.VMEM((2, n_pool, rows // 2, width), bf16),
             dma((6,)), dma((3, 4)),
             dma((2, far)), dma((2, far)), dma((3,)), dma((3,)), dma((far,)), dma((far,)),
-            dma((3, 2)), dma((3, 2)), dma((3,)), dma((3,)),
-            dma((width // 512, far)), dma((width // 512, far)),
+            dma((2, 3, 2)), dma((2, 3, 2)), dma((2, 3)), dma((2, 3)),
+            dma((2, 2, far)), dma((2, 2, far)),
         ],
         compiler_params=pltpu.CompilerParams(
             collective_id=0, has_side_effects=True, vmem_limit_bytes=VMEM_BYTES
@@ -424,7 +477,7 @@
         and n_sub == 2
         and n_pool > 1
         and rows % 32 == 0
-        and width % 512 == 0
+        and width % 1024 == 0
         and unit_width % (4 * HEAD_DIM) == 0
         and weight_bytes + 4 * cache_keys.size + 24 * n_pool * rows * unit_width
         <= VMEM_BYTES

time: 58.1 us -> 52.1 us (0.90)
  Pallas kernels: 56.2 us -> 50.2 us
    pallas_call x1, Pallas kernels: 56.2 us -> 50.2 us  [fused_rows(): pl.pallas_call(functools.partial(fused_kernel, n_pool), out_shape=jax.Sha...]
where the time goes in v2:
time: 52.1 us; the launch traced here: 51.8 us
  Pallas kernels  50.2 us (96%)
  local copies, waits for them, and re-layouts  1.67 us (3%)
    pallas_call x1, Pallas kernels, fused_rows(): pl.pallas_call(functools.partial(fused_kernel, n_pool), out_shape=jax.Sha...  50.2 us
    unnamed x1, local copies, waits for them, and re-layouts  1.67 us

profile of v2, /device:TPU:0, one launch (start us, length us, event | category | flops | bytes accessed | tf_op | source)
XLA Modules:
  0.0 51.8 jit_solution(7406867680965558878)
XLA Ops:
  0.0 50.2 %shard_map.109 = f32[32,2048]{1,0:T(8,128)} custom-call(bf16[32,2048]{1,0:T(8,128)(2,1)} %q_hbm.1, bf16[32,128,256]{2,1,0:T(8,128)(2,1)} %k_hbm.1, bf16[32,128,256]{2,1,0:T(8,128)(2,1)} %v_hbm.1, bf16[32,256]{1,0:T(8,128)(2,1)} %nk_ref.1, bf16[32,256]{1,0:T(8,128)(2,1)} %nv_ref.1, s32[32]{0:T(128)} %len_ref.1, f32[32,2048]{1,0:T(8,128)} %res_hbm.1, ...), custom_call_target="tpu_custom_call" | custom-call | tf_op jit(solution)/shard_map/pallas_call | solution.py:434
  50.2 1.7 %copy.13 = f32[32,2048]{1,0:T(8,128)} copy(f32[32,2048]{1,0:T(8,128)} %shard_map.109) | data formatting | bytes 524288

commit v3 on v2

--- a/solution.py
+++ b/solution.py
@@ -119,7 +119,10 @@
     f = lax.axis_index("ffn")
     s = lax.axis_index("sub")
     me = f * 2 + s
-    pool_at = [lax.rem(p + d, n_pool) for d in range(1, n_pool)]
+    if n_pool == 4:
+        pool_at = [3 - p, lax.rem(p + 2, 4), p + 1 - 2 * lax.rem(p, 2)]
+    else:
+        pool_at = [lax.rem(p + d, n_pool) for d in range(1, n_pool)]
     sibling = {"sub": 1 - s}
     across = {"ffn": 1 - f}
     diagonal = {"ffn": 1 - f, "sub": 1 - s}

time: 52.1 us -> 51.8 us (level)
  no operation moved by 1% of the time
where the time goes in v3:
time: 51.8 us; the launch traced here: 51.6 us
  Pallas kernels  49.9 us (96%)
  local copies, waits for them, and re-layouts  1.67 us (3%)
    pallas_call x1, Pallas kernels, fused_rows(): pl.pallas_call(functools.partial(fused_kernel, n_pool), out_shape=jax.Sha...  49.9 us
    unnamed x1, local copies, waits for them, and re-layouts  1.67 us

profile of v3, /device:TPU:0, one launch (start us, length us, event | category | flops | bytes accessed | tf_op | source)
XLA Modules:
  0.0 51.6 jit_solution(4843669553268105242)
XLA Ops:
  0.0 49.9 %shard_map.109 = f32[32,2048]{1,0:T(8,128)} custom-call(bf16[32,2048]{1,0:T(8,128)(2,1)} %q_hbm.1, bf16[32,128,256]{2,1,0:T(8,128)(2,1)} %k_hbm.1, bf16[32,128,256]{2,1,0:T(8,128)(2,1)} %v_hbm.1, bf16[32,256]{1,0:T(8,128)(2,1)} %nk_ref.1, bf16[32,256]{1,0:T(8,128)(2,1)} %nv_ref.1, s32[32]{0:T(128)} %len_ref.1, f32[32,2048]{1,0:T(8,128)} %res_hbm.1, ...), custom_call_target="tpu_custom_call" | custom-call | tf_op jit(solution)/shard_map/pallas_call | solution.py:437
  49.9 1.7 %copy.13 = f32[32,2048]{1,0:T(8,128)} copy(f32[32,2048]{1,0:T(8,128)} %shard_map.109) | data formatting | bytes 524288
